TPU v7x, 512 devices: a whole 4x8x8 slice. The times are simulated.
512 devices in a mesh: seq: 128 (over y, z, core), fsdp: 4 (over x).
Axes of the slice: x: 4, y: 8, z: 8, core: 2. Of those that a mesh axis runs over, the one named last changes fastest.
Arguments:
- tokens: bfloat16 [4, 16384, 2048], P('fsdp', 'seq'), may hold values from -14 to 14
- w_qkv: bfloat16 [2048, 3, 1024], P(None, None, 'fsdp'), may hold values from -0.125 to 0.125
- w_feature: bfloat16 [8, 128, 16], replicated, may hold values from -2 to 2
- norm_gain: float32 [1024], replicated, may hold values from 0.5 to 1.5
- log_decay: float32 [4, 8, 16384], P('fsdp', None, 'seq'), may hold values from -1.5 to 0
- pattern: int32 [4, 256, 3], P('fsdp', 'seq'), may hold values from 1 to 255, as said below
Outputs:
- mixed: bfloat16 [4, 16384, 1024], P('fsdp', 'seq')
Inputs may be any that keep to these rules, and one draw needn't show every extreme that they name: `pattern`: the 3 blocks of query block b are distinct, none is among the first 1 block or equal to b - 1, b or b + 1, and each lies in a segment at most 3 segments from b's segment; the first lies exactly 3 segments later where that segment exists, else 3 segments earlier.
All inputs are finite; a program needn't handle non-finite values.
Results may differ from a plain program's by a relative error of at most 0.0097.
The roundings to bfloat16 on the way count: a program that leaves them out, or rounds other values in their place, can miss the bound.
Values may be sent and summed in bfloat16 or wider, within the bound.
No kernel may reach another device: no remote copies, remote signals or barrier semaphores. Data moves between devices by JAX's collectives and lax.ppermute only.
A program may use at most 64 MiB of HBM per device.

v0:
```python
import jax
import jax.numpy as jnp
from jax import lax
from jax.sharding import PartitionSpec as P

HALF_HEADS = 8
DH = 128
F = 16
HD = 1024
BS = 64
G = 1
R = 3
RD = 3
TOK_DEV = 128
NB_DEV = 2
epsilon = 1e-06
masked_score = -1e30


def from_behind(value, axis, steps):
    count = lax.axis_size(axis)
    initial, last = (max(0, -steps), min(count, count - steps))
    return lax.ppermute(value, axis, [(source, source + steps) for source in range(initial, last)])


def spread(array, axis, root):
    mine = lax.axis_index(axis) == root
    return lax.psum(jnp.where(mine, array, jnp.zeros_like(array)), axis)


def entering(value, axis, join, neutral):
    count, mine = (lax.axis_size(axis), lax.axis_index(axis))
    pieces = jax.tree.map(lambda part: lax.all_gather(part, axis), value)
    running = jax.tree.map(
        lambda part, zero: jnp.full_like(part, 0) + jnp.asarray(zero, part.dtype), value, neutral
    )

    def lap(position, running):
        longer = join(running, jax.tree.map(lambda part: part[position], pieces))
        return jax.tree.map(lambda new, old: jnp.where(position < mine, new, old), longer, running)

    return lax.fori_loop(0, count - 1, lap, running)


def feature_map(projected_head, w_feature):
    logits = jnp.einsum(
        "thd,hdf->htf", projected_head, w_feature, preferred_element_type=jnp.float32
    )
    return jax.nn.softmax(logits, axis=-1).astype(jnp.bfloat16)


def combine_states(earlier, following):
    return (earlier[0] * following[0], following[0][:, None, None] * earlier[1] + following[1])


def neighbour_piece(pair_rows, offset):
    return from_behind(pair_rows, "seq", -offset)


def per_device(tokens, w_qkv, w_feature, norm_gain, log_decay, pattern):
    projected = jnp.einsum(
        "btd,dkc->btkc",
        tokens,
        lax.all_gather(w_qkv, "fsdp", axis=2, tiled=True),
        preferred_element_type=jnp.float32,
    ).astype(jnp.bfloat16)
    queries = projected[0, :, 0].reshape(TOK_DEV, HALF_HEADS, DH)
    key_rows = projected[0, :, 1].reshape(TOK_DEV, HALF_HEADS, DH)
    values = projected[0, :, 2].reshape(TOK_DEV, HALF_HEADS, DH)
    pair_rows = projected[:, :, 1:3].reshape(1, TOK_DEV, 2 * HD)
    pieces = []
    for offset in range(-RD, RD + 1):
        if offset == 0:
            pieces.append(pair_rows)
        else:
            pieces.append(neighbour_piece(pair_rows, offset))
    region = jnp.concatenate(pieces, axis=1)
    global_rows = spread(pair_rows[0, : G * BS], "seq", 0)
    phi_query = feature_map(queries, w_feature)
    phi_key = feature_map(key_rows, w_feature)
    log_steps = log_decay[0]
    cumulative = jnp.cumsum(log_steps, axis=1)
    final_log = cumulative[:, -1:]
    weighted_key = (
        jnp.exp(final_log - cumulative)[:, :, None] * phi_key.astype(jnp.float32)
    ).astype(jnp.bfloat16)
    local_state = jnp.einsum(
        "htf,thd->hfd", weighted_key, values, preferred_element_type=jnp.float32
    )
    identity = (jnp.ones((HALF_HEADS,), jnp.float32), jnp.zeros((HALF_HEADS, F, DH), jnp.float32))
    carried_pair = entering(
        (jnp.exp(final_log[:, 0]), local_state), "seq", combine_states, identity
    )
    carried = carried_pair[1]
    scores = jnp.einsum("htf,hsf->hts", phi_query, phi_key, preferred_element_type=jnp.float32)
    log_gap = cumulative[:, :, None] - cumulative[:, None, :]
    causal = jnp.arange(TOK_DEV)[:, None] >= jnp.arange(TOK_DEV)[None, :]
    decay_matrix = jnp.where(causal[None], jnp.exp(jnp.minimum(log_gap, 0.0)), 0.0)
    mixing = (scores * decay_matrix).astype(jnp.bfloat16)
    local_term = jnp.einsum("hts,shd->thd", mixing, values, preferred_element_type=jnp.float32)
    carried_term = jnp.einsum(
        "htf,hfd->thd", phi_query.astype(jnp.float32), carried, precision=lax.Precision.HIGHEST
    )
    carried_term = carried_term * jnp.exp(cumulative).T[:, :, None]
    linear = local_term + carried_term
    normed = linear * lax.rsqrt(jnp.mean(linear * linear, axis=-1, keepdims=True) + epsilon)
    normed = normed * norm_gain.reshape(HALF_HEADS, DH)
    device = lax.axis_index("seq")
    block_total = lax.axis_size("seq") * NB_DEV
    window_blocks = region[0].reshape((2 * RD + 1) * NB_DEV, BS, 2 * HD)
    query_blocks = device * NB_DEV + jnp.arange(NB_DEV, dtype=jnp.int32)
    near_blocks = query_blocks[:, None] + jnp.arange(-1, 2, dtype=jnp.int32)[None, :]
    usable_near = (near_blocks >= G) & (near_blocks < block_total)
    chosen = jnp.concatenate([near_blocks, pattern[0]], axis=1) - (device - RD) * NB_DEV
    chosen = jnp.clip(chosen, 0, (2 * RD + 1) * NB_DEV - 1)
    usable = jnp.concatenate([usable_near, jnp.ones((NB_DEV, R), dtype=bool)], axis=1)
    usable_keys = jnp.repeat(usable, BS, axis=1)
    picked = jnp.take(window_blocks, chosen, axis=0).reshape(
        NB_DEV, (3 + R) * BS, 2, HALF_HEADS, DH
    )
    global_split = global_rows.reshape(G * BS, 2, HALF_HEADS, DH)
    query_rows = queries.reshape(NB_DEV, BS, HALF_HEADS, DH)
    score_scale = DH ** (-0.5)
    near_scores = (
        jnp.einsum(
            "nqhd,nkhd->nhqk", query_rows, picked[:, :, 0], preferred_element_type=jnp.float32
        )
        * score_scale
    )
    near_scores = jnp.where(usable_keys[:, None, None, :], near_scores, masked_score)
    far_scores = (
        jnp.einsum(
            "nqhd,khd->nhqk", query_rows, global_split[:, 0], preferred_element_type=jnp.float32
        )
        * score_scale
    )
    scores_all = jnp.concatenate([near_scores, far_scores], axis=-1)
    highest = jnp.max(scores_all, axis=-1, keepdims=True)
    exponent = jnp.exp(scores_all - highest)
    denominator = jnp.sum(exponent, axis=-1, keepdims=True)
    soft_weights = (exponent / denominator).astype(jnp.bfloat16)
    near_count = (3 + R) * BS
    sparse = jnp.einsum(
        "nhqk,nkhd->nqhd",
        soft_weights[..., :near_count],
        picked[:, :, 1],
        preferred_element_type=jnp.float32,
    )
    sparse = sparse + jnp.einsum(
        "nhqk,khd->nqhd",
        soft_weights[..., near_count:],
        global_split[:, 1],
        preferred_element_type=jnp.float32,
    )
    sparse = sparse.reshape(TOK_DEV, HALF_HEADS, DH)
    return (normed + sparse).astype(jnp.bfloat16).reshape(1, TOK_DEV, HD)


def solution(mesh):
    placed = (
        P("fsdp", "seq", None),
        P(None, None, "fsdp"),
        P(),
        P(),
        P("fsdp", None, "seq"),
        P("fsdp", "seq", None),
    )
    return jax.shard_map(
        per_device, mesh=mesh, in_specs=placed, out_specs=P("fsdp", "seq", None), check_vma=False
    )
```

profile of v0, /device:TPU:9, one launch (start us, length us, event | category | flops | bytes accessed | tf_op | source)
XLA Modules:
  0.0 615.5 jit_solution(8857086100503208488)
XLA Ops:
  7.9 133.5 %all-gather.5.cloned.1.call-done = bf16[2048,3,1024]{2,0,1:T(8,128)(2,1)} async-done(((bf16[2048,3,256]{2,0,1:T(8,128)(2,1)}), bf16[2048,3,1024]{2,0,1:T(8,128)(2,1)}) %all-gather.5.cloned.1.call-update) | async-done | bytes 12582928 | tf_op jit(solution)/shard_map/all_gather | solution.py:64
  141.4 6.4 %fusion.7 = bf16[1,128,3,1024]{3,1,2,0:T(8,128)(2,1)S(1)} fusion(bf16[2048,3,1024]{2,0,1:T(8,128)(2,1)} %all-gather.5.cloned.1.call-done, bf16[1,128,2048]{2,1,0:T(8,128)(2,1)S(1)} %copy-done), kind=kOutput, calls=%fused_computation.17 | convolution fusion | flops 1611005952 | bytes 13893632 | tf_op jit(solution)/shard_map/btd,dkc->btkc/dot_general | solution.py:61
  151.9 1.3 dynamic-slice
  154.0 213.7 %all-reduce.1 = f32[1024]{0:T(1024)S(1)} all-reduce(f32[1024]{0:T(1024)S(1)} %dynamic-update-slice), channel_id=2, replica_groups=mesh['seq'=128,'fsdp'=4] {'seq'}, use_global_device_ids=true, to_apply=%add.1 | all-reduce | flops 1024 | bytes 8192
  368.4 1.9 collective-permute-start
  370.3 1.9 collective-permute-start.1
  372.3 2.1 collective-permute-start.2
  374.3 5.9 collective-permute-start.3
  380.2 7.2 %collective-permute-start.4 = (bf16[1,128,2048]{1,2,0:T(8,128)(2,1)S(1)}, bf16[1,128,2048]{1,2,0:T(8,128)(2,1)S(1)}, u32[]{:S(2)}, u32[]{:S(2)}) collective-permute-start(bf16[1,128,2048]{1,2,0:T(8,128)(2,1)S(1)} %bitcast.123), channel_id=1, source_target_pairs={{8,0},{12,4},{16,8},{20,12},{24,16},{28,20},{32,24},{36,28},{40,32... | collective-permute-start | bytes 1572872 | tf_op jit(solution)/shard_map/ppermute | solution.py:23
  388.0 1.1 fusion.37
  389.4 8.5 %collective-permute-done = bf16[1,128,2048]{1,2,0:T(8,128)(2,1)} collective-permute-done((bf16[1,128,2048]{1,2,0:T(8,128)(2,1)S(1)}, bf16[1,128,2048]{1,2,0:T(8,128)(2,1)}, u32[]{:S(2)}, u32[]{:S(2)}) %collective-permute-start) | collective-permute-done | bytes 524320 | tf_op jit(solution)/shard_map/ppermute | solution.py:23
  397.9 3.3 collective-permute-start.5
  401.2 1.9 constant_dynamic-update-slice_fusion.6
  403.1 1.9 constant_dynamic-update-slice_fusion.5
  405.4 1.9 constant_dynamic-update-slice_fusion.4
  408.2 1.0 constant_dynamic-update-slice_fusion.2
  410.1 3.3 collective-permute-done.5
  414.2 6.2 %copy.54 = bf16[1,896,2048]{2,1,0:T(8,128)(2,1)} copy(bf16[1,896,2048]{1,2,0:T(8,128)(2,1)} %constant_dynamic-update-slice_fusion) | data formatting | bytes 7340032 | tf_op jit(solution)/shard_map/concatenate | solution.py:77
  420.4 4.6 gather_fusion
  425.0 2.9 copy.70
  432.0 52.2 %all-gather.7.cloned.1.call-done = f32[1024,16,128]{2,1,0:T(8,128)} async-done(((f32[8,16,128]{2,1,0:T(8,128)}), f32[1024,16,128]{2,1,0:T(8,128)}) %all-gather.7.cloned.1.call-update) | async-done | bytes 8388624 | tf_op jit(solution)/shard_map/all_gather | solution.py:33
  484.2 122.4 %while.14 = (s32[]{:T(128)}, f32[8,16,128]{2,1,0:T(8,128)S(1)}, s32[]{:T(128)}, f32[128,8]{1,0:T(8,128)S(1)}, f32[128,8,16,128]{3,2,1,0:T(8,128)}, /*index=5*/s32[]{:T(128)}, s32[]{:T(128)}) while((s32[]{:T(128)}, f32[8,16,128]{2,1,0:T(8,128)S(1)}, s32[]{:T(128)}, f32[128,8]{1,0:T(8,128)S(1)}, f32[128,8,16,128]{3,2,1,0:T(8,128)}, ...), condition=%wide.region_6.7_spmd.clone, body=%wide.region_5.6_spmd.clone.sunk | while | flops 65540 | bytes 196809 | solution.py:42
  485.2 0.9 fusion.58
  486.1 0.9 fusion.58
  487.1 0.9 fusion.58
  488.1 0.9 fusion.58
  489.0 0.9 fusion.58
  491.0 0.9 fusion.58
  492.9 0.9 fusion.58
  493.8 0.9 fusion.58
  494.8 0.9 fusion.58
  495.8 0.9 fusion.58
  496.7 0.9 fusion.58
  497.7 0.9 fusion.58
  498.7 0.9 fusion.58
  499.6 0.9 fusion.58
  500.6 0.9 fusion.58
  501.6 0.9 fusion.58
  502.5 0.9 fusion.58
  503.5 0.9 fusion.58
  504.4 0.9 fusion.58
  505.4 0.9 fusion.58
  506.4 0.9 fusion.58
  507.3 0.9 fusion.58
  509.3 0.9 fusion.58
  511.2 0.9 fusion.58
  512.2 0.9 fusion.58
  513.1 0.9 fusion.58
  514.1 0.9 fusion.58
  515.1 0.9 fusion.58
  516.0 0.9 fusion.58
  517.0 0.9 fusion.58
  517.9 0.9 fusion.58
  518.9 0.9 fusion.58
  519.9 0.9 fusion.58
  520.8 0.9 fusion.58
  521.8 0.9 fusion.58
  522.8 0.9 fusion.58
  523.7 0.9 fusion.58
  524.7 0.9 fusion.58
  525.7 0.9 fusion.58
  527.6 0.9 fusion.58
  529.5 0.9 fusion.58
  530.5 0.9 fusion.58
  (301 shorter events, 95.9 us)
Async XLA Ops:
  6.5 134.9 %copy-start = (bf16[1,128,2048]{2,1,0:T(8,128)(2,1)S(1)}, bf16[1,128,2048]{2,1,0:T(8,128)(2,1)}, u32[]{:S(2)}) copy-start(bf16[1,128,2048]{2,1,0:T(8,128)(2,1)} %param.8) | copy-start | bytes 1572868
  6.5 0.8 copy-start.6
  6.5 134.9 %all-gather.5.cloned.1.call-start = ((), (), s32[]{:S(2)}) async-start(), calls=%async_computation | async-start | bytes 15728640 | tf_op jit(solution)/shard_map/all_gather | solution.py:64
  7.3 380.8 %all-reduce.4.cloned.1.call-start = ((), (), s32[]{:S(2)}) async-start(), calls=%async_computation.1 | async-start | bytes 524288 | tf_op jit(solution)/shard_map/psum | solution.py:28
  147.8 1.5 copy-start.7
  147.8 2.8 copy-start.5
  149.2 335.0 %all-gather.7.cloned.1.call-start = ((), (), s32[]{:S(2)}) async-start(), calls=%async_computation.2 | async-start | bytes 8454144 | tf_op jit(solution)/shard_map/all_gather | solution.py:33
  149.5 237.9 %copy-start.8 = (f32[8,128,16]{1,2,0:T(8,128)}, f32[8,128,16]{1,2,0:T(8,128)S(1)}, u32[]{:S(2)}) copy-start(f32[8,128,16]{1,2,0:T(8,128)S(1)} %fusion.26) | copy-start | bytes 196612
  149.6 0.9 copy-start.10
  368.4 29.5 %collective-permute-start = (bf16[1,128,2048]{1,2,0:T(8,128)(2,1)S(1)}, bf16[1,128,2048]{1,2,0:T(8,128)(2,1)}, u32[]{:S(2)}, u32[]{:S(2)}) collective-permute-start(bf16[1,128,2048]{1,2,0:T(8,128)(2,1)S(1)} %bitcast.119), channel_id=1, source_target_pairs={{0,12},{4,16},{8,20},{12,24},{16,28},{20,32},{24,36},{28,40},{32,4... | collective-permute-start | bytes 1572872 | tf_op jit(solution)/shard_map/ppermute | solution.py:23
  370.3 32.8 %collective-permute-start.1 = (bf16[1,128,2048]{1,2,0:T(8,128)(2,1)S(1)}, bf16[1,128,2048]{1,2,0:T(8,128)(2,1)}, u32[]{:S(2)}, u32[]{:S(2)}) collective-permute-start(bf16[1,128,2048]{1,2,0:T(8,128)(2,1)S(1)} %bitcast.120), channel_id=1, source_target_pairs={{0,8},{4,12},{8,16},{12,20},{16,24},{20,28},{24,32},{28,36},{32,40... | collective-permute-start | bytes 1572872 | tf_op jit(solution)/shard_map/ppermute | solution.py:23
  372.3 33.1 %collective-permute-start.2 = (bf16[1,128,2048]{1,2,0:T(8,128)(2,1)S(1)}, bf16[1,128,2048]{1,2,0:T(8,128)(2,1)}, u32[]{:S(2)}, u32[]{:S(2)}) collective-permute-start(bf16[1,128,2048]{1,2,0:T(8,128)(2,1)S(1)} %bitcast.121), channel_id=1, source_target_pairs={{0,4},{4,8},{8,12},{12,16},{16,20},{20,24},{24,28},{28,32},{32,36}... | collective-permute-start | bytes 1572872 | tf_op jit(solution)/shard_map/ppermute | solution.py:23
  374.3 33.8 %collective-permute-start.3 = (bf16[1,128,2048]{1,2,0:T(8,128)(2,1)S(1)}, bf16[1,128,2048]{1,2,0:T(8,128)(2,1)S(1)}, u32[]{:S(2)}, u32[]{:S(2)}) collective-permute-start(bf16[1,128,2048]{1,2,0:T(8,128)(2,1)S(1)} %bitcast.122), channel_id=1, source_target_pairs={{4,0},{8,4},{12,8},{16,12},{20,16},{24,20},{28,24},{32,28},{36,32}... | collective-permute-start | bytes 1572872 | tf_op jit(solution)/shard_map/ppermute | solution.py:23
  380.2 28.9 %collective-permute-start.4 = (bf16[1,128,2048]{1,2,0:T(8,128)(2,1)S(1)}, bf16[1,128,2048]{1,2,0:T(8,128)(2,1)S(1)}, u32[]{:S(2)}, u32[]{:S(2)}) collective-permute-start(bf16[1,128,2048]{1,2,0:T(8,128)(2,1)S(1)} %bitcast.123), channel_id=1, source_target_pairs={{8,0},{12,4},{16,8},{20,12},{24,16},{28,20},{32,24},{36,28},{40,32... | collective-permute-start | bytes 1572872 | tf_op jit(solution)/shard_map/ppermute | solution.py:23
  397.9 15.4 %collective-permute-start.5 = (bf16[1,128,2048]{1,2,0:T(8,128)(2,1)S(1)}, bf16[1,128,2048]{1,2,0:T(8,128)(2,1)S(1)}, u32[]{:S(2)}, u32[]{:S(2)}) collective-permute-start(bf16[1,128,2048]{1,2,0:T(8,128)(2,1)S(1)} %bitcast.124), channel_id=1, source_target_pairs={{12,0},{16,4},{20,8},{24,12},{28,16},{32,20},{36,24},{40,28},{44,3... | collective-permute-start | bytes 1572872 | tf_op jit(solution)/shard_map/ppermute | solution.py:23
  427.9 0.8 copy-start.3
  430.3 1.0 copy-start.1
  431.2 176.0 %copy-start.2 = (pred[128,128]{1,0:T(8,128)(4,1)S(1)}, pred[128,128]{1,0:T(8,128)(4,1)}, u32[]{:S(2)}) copy-start(pred[128,128]{1,0:T(8,128)(4,1)} %iota_compare_fusion) | copy-start | bytes 49156
  431.3 176.0 %copy-start.9 = (f32[8,128,16]{1,2,0:T(8,128)S(1)}, f32[8,128,16]{1,2,0:T(8,128)}, u32[]{:S(2)}) copy-start(f32[8,128,16]{1,2,0:T(8,128)} %copy-done.8) | copy-start | bytes 196612
  431.3 176.0 %copy-start.11 = (f32[8,128]{1,0:T(8,128)S(1)}, f32[8,128]{1,0:T(8,128)}, u32[]{:S(2)}) copy-start(f32[8,128]{1,0:T(8,128)} %copy-done.10) | copy-start | bytes 12292
  431.5 176.4 %copy-start.4 = (f32[1024]{0:T(1024)S(1)}, f32[1024]{0:T(1024)}, u32[]{:S(2)}) copy-start(f32[1024]{0:T(1024)} %param.11) | copy-start | bytes 12292
Sparse Core Ops, SparseCore 0:
  9.5 131.8 all-gather.4
  149.3 190.4 all-reduce.3
  342.9 141.2 all-gather.6
where the time goes:
time: 622 us; the launch traced here: 615 us
  blocking collectives  214 us (34%)
  waiting for transfers between devices  199 us (32%)
  other arithmetic  121 us (19%)
  local copies, waits for them, and re-layouts  30.1 us (5%)
  starting transfers between devices  22.4 us (4%)
  between operations  14.2 us (2%)
  matrix products  11.5 us (2%)
    unnamed x1, blocking collectives  214 us
    all_gather x1, waiting for transfers between devices, per_device(): lax.all_gather(w_qkv, 'fsdp', axis=2, tiled=True)  134 us
    select_n x127, other arithmetic, lap(): jnp.where(position < mine, new, old)  117 us
    all_gather x1, waiting for transfers between devices, entering(): pieces = jax.tree.map(lambda part: lax.all_gather(part, axis), value)  52.2 us
    ppermute x6, starting transfers between devices, from_behind(): lax.ppermute(value, axis, [(source, source + steps) for source in range(i...  22.3 us
    unnamed x38, local copies, waits for them, and re-layouts  13.2 us
  transfers between devices with their start and end apart: 9, of which 5 were waited for; matrix products, arithmetic and copies ran while one was open for 6% of the time, Pallas kernels for 0%

commit v1 on v0

--- a/solution.py
+++ b/solution.py
@@ -61,7 +61,9 @@
     projected = jnp.einsum(
         "btd,dkc->btkc",
         tokens,
-        lax.all_gather(w_qkv, "fsdp", axis=2, tiled=True),
+        jnp.concatenate(
+            lax.all_to_all(jnp.stack([w_qkv] * lax.axis_size("fsdp")), "fsdp", 0, 0), axis=2
+        ),
         preferred_element_type=jnp.float32,
     ).astype(jnp.bfloat16)
     queries = projected[0, :, 0].reshape(TOK_DEV, HALF_HEADS, DH)

time: 622 us -> 736 us (1.18)
  the two profiles are of different devices: /device:TPU:9 before, /device:TPU:32 now
where the time goes in v1:
time: 736 us; the launch traced here: 726 us
  blocking collectives  254 us (35%)
  waiting for transfers between devices  171 us (23%)
  local copies, waits for them, and re-layouts  131 us (18%)
  other arithmetic  120 us (16%)
  starting transfers between devices  25.3 us (3%)
  between operations  14.6 us (2%)
    unnamed x1, blocking collectives  254 us
    all_to_all x1, waiting for transfers between devices, per_device(): lax.all_to_all(jnp.stack([w_qkv] * lax.axis_size('fsdp')), 'fsdp', 0, 0)  138 us
    select_n x127, other arithmetic, lap(): jnp.where(position < mine, new, old)  117 us
    mul x127, local copies, waits for them, and re-layouts, combine_states(): following[0][:, None, None] * earlier[1] + following[1]  87.3 us
    ppermute x6, waiting for transfers between devices, from_behind(): lax.ppermute(value, axis, [(source, source + steps) for source in range(i...  32.1 us
    ppermute x6, starting transfers between devices, from_behind(): lax.ppermute(value, axis, [(source, source + steps) for source in range(i...  18.7 us
  transfers between devices with their start and end apart: 9, of which 6 were waited for; matrix products, arithmetic and copies ran while one was open for 5% of the time, Pallas kernels for 0%

profile of v1, /device:TPU:32, one launch (start us, length us, event | category | flops | bytes accessed | tf_op | source)
XLA Modules:
  0.0 725.6 jit_solution(2145646538984858502)
XLA Ops:
  6.5 7.5 %stack.2 = bf16[4,2048,3,256]{3,1,2,0:T(8,128)(2,1)} broadcast(bf16[2048,3,256]{2,0,1:T(8,128)(2,1)} %param.9), dimensions={1,2,3} | broadcast | bytes 15728640 | tf_op jit(solution)/shard_map/stack | solution.py:65
  14.0 6.5 all-to-all-start
  21.1 138.4 %all-to-all-done = bf16[4,2048,3,256]{3,1,2,0:T(8,128)(2,1)} async-done(((bf16[4,2048,3,256]{3,1,2,0:T(8,128)(2,1)}), bf16[4,2048,3,256]{3,1,2,0:T(8,128)(2,1)}, u32[]{:S(2)}, u32[]{:S(2)}) %all-to-all-start) | async-done | bytes 12582944 | tf_op jit(solution)/shard_map/all_to_all | solution.py:65
  159.5 6.6 copy.67
  166.1 1.8 fusion.7
  172.5 1.3 dynamic-slice
  174.8 254.4 %all-reduce.1 = f32[1024]{0:T(1024)S(1)} all-reduce(f32[1024]{0:T(1024)S(1)} %dynamic-update-slice), channel_id=2, replica_groups=mesh['seq'=128,'fsdp'=4] {'seq'}, use_global_device_ids=true, to_apply=%add.1 | all-reduce | flops 1024 | bytes 8192
  430.5 1.9 collective-permute-start
  432.4 1.9 collective-permute-start.1
  434.4 1.9 collective-permute-start.2
  436.3 7.0 collective-permute-start.3
  443.3 3.9 collective-permute-start.4
  448.2 1.1 fusion.37
  449.6 1.7 collective-permute-done
  451.3 2.1 collective-permute-start.5
  453.4 1.9 constant_dynamic-update-slice_fusion.6
  455.3 8.1 %collective-permute-done.1 = bf16[1,128,2048]{1,2,0:T(8,128)(2,1)} collective-permute-done((bf16[1,128,2048]{1,2,0:T(8,128)(2,1)S(1)}, bf16[1,128,2048]{1,2,0:T(8,128)(2,1)}, u32[]{:S(2)}, u32[]{:S(2)}) %collective-permute-start.1) | collective-permute-done | bytes 524320 | tf_op jit(solution)/shard_map/ppermute | solution.py:23
  463.3 1.9 constant_dynamic-update-slice_fusion.5
  465.3 3.0 collective-permute-done.2
  470.0 1.0 constant_dynamic-update-slice_fusion.2
  471.0 1.8 collective-permute-done.4
  473.8 17.5 %collective-permute-done.5 = bf16[1,128,2048]{1,2,0:T(8,128)(2,1)S(1)} collective-permute-done((bf16[1,128,2048]{1,2,0:T(8,128)(2,1)S(1)}, bf16[1,128,2048]{1,2,0:T(8,128)(2,1)S(1)}, u32[]{:S(2)}, u32[]{:S(2)}) %collective-permute-start.5) | collective-permute-done | bytes 524320 | tf_op jit(solution)/shard_map/ppermute | solution.py:23
  492.2 6.2 copy.55
  498.4 4.7 gather_fusion
  503.1 2.9 copy.72
  510.1 206.2 %while.14 = (s32[]{:T(128)}, f32[8,16,128]{2,1,0:T(8,128)S(1)}, s32[]{:T(128)}, f32[128,8]{1,0:T(8,128)}, f32[128,8,16,128]{3,2,1,0:T(8,128)}, /*index=5*/s32[]{:T(128)}, s32[]{:T(128)}) while((s32[]{:T(128)}, f32[8,16,128]{2,1,0:T(8,128)S(1)}, s32[]{:T(128)}, f32[128,8]{1,0:T(8,128)}, f32[128,8,16,128]{3,2,1,0:T(8,128)}, ...), condition=%wide.region_6.7_spmd.clone, body=%wide.region_5.6_spmd.clone.sunk | while | flops 65540 | bytes 196809 | solution.py:42
  510.9 0.9 fusion.58
  514.1 0.9 fusion.58
  515.8 0.9 fusion.58
  519.0 0.9 fusion.58
  523.9 0.9 fusion.58
  525.5 0.9 fusion.58
  527.1 0.9 fusion.58
  535.3 0.9 fusion.58
  536.9 0.9 fusion.58
  541.7 0.9 fusion.58
  548.2 0.9 fusion.58
  553.1 0.9 fusion.58
  557.9 0.9 fusion.58
  562.8 0.9 fusion.58
  564.4 0.9 fusion.58
  567.6 0.9 fusion.58
  569.3 0.9 fusion.58
  574.1 0.9 fusion.58
  575.7 0.9 fusion.58
  577.4 0.9 fusion.58
  579.0 0.9 fusion.58
  580.6 0.9 fusion.58
  582.2 0.9 fusion.58
  583.8 0.9 fusion.58
  585.5 0.9 fusion.58
  587.1 0.9 fusion.58
  588.7 0.9 fusion.58
  590.3 0.9 fusion.58
  601.7 0.9 fusion.58
  603.4 0.9 fusion.58
  605.0 0.9 fusion.58
  606.6 0.9 fusion.58
  608.2 0.9 fusion.58
  609.9 0.9 fusion.58
  611.5 0.9 fusion.58
  613.1 0.9 fusion.58
  614.8 0.9 fusion.58
  616.4 0.9 fusion.58
  (310 shorter events, 186.5 us)
Async XLA Ops:
  6.5 159.6 %copy-start = (bf16[1,128,2048]{2,1,0:T(8,128)(2,1)S(1)}, bf16[1,128,2048]{2,1,0:T(8,128)(2,1)}, u32[]{:S(2)}) copy-start(bf16[1,128,2048]{2,1,0:T(8,128)(2,1)} %param.8) | copy-start | bytes 1572868
  14.0 6.5 copy-start.10
  14.0 145.5 %all-to-all-start = ((bf16[4,2048,3,256]{3,1,2,0:T(8,128)(2,1)}), bf16[4,2048,3,256]{3,1,2,0:T(8,128)(2,1)}, u32[]{:S(2)}, u32[]{:S(2)}) async-start(bf16[4,2048,3,256]{3,1,2,0:T(8,128)(2,1)} %stack.2), calls=%async_computation | async-start | bytes 25165824 | tf_op jit(solution)/shard_map/all_to_all | solution.py:65
  20.5 427.3 %all-reduce.4.cloned.1.call-start = ((), (), s32[]{:S(2)}) async-start(), calls=%async_computation.1 | async-start | bytes 524288 | tf_op jit(solution)/shard_map/psum | solution.py:28
  167.9 1.5 copy-start.11
  168.0 2.7 copy-start.9
  169.3 340.8 %all-gather.4.cloned.1.call-start = ((), (), s32[]{:S(2)}) async-start(), calls=%async_computation.2 | async-start | bytes 8454144 | tf_op jit(solution)/shard_map/all_gather | solution.py:33
  169.7 277.6 %copy-start.12 = (f32[8,128,16]{1,2,0:T(8,128)}, f32[8,128,16]{1,2,0:T(8,128)S(1)}, u32[]{:S(2)}) copy-start(f32[8,128,16]{1,2,0:T(8,128)S(1)} %fusion.26) | copy-start | bytes 196612
  169.7 1.2 copy-start.14
  430.5 20.8 %collective-permute-start = (bf16[1,128,2048]{1,2,0:T(8,128)(2,1)S(1)}, bf16[1,128,2048]{1,2,0:T(8,128)(2,1)}, u32[]{:S(2)}, u32[]{:S(2)}) collective-permute-start(bf16[1,128,2048]{1,2,0:T(8,128)(2,1)S(1)} %bitcast.123), channel_id=1, source_target_pairs={{0,12},{4,16},{8,20},{12,24},{16,28},{20,32},{24,36},{28,40},{32,4... | collective-permute-start | bytes 1572872 | tf_op jit(solution)/shard_map/ppermute | solution.py:23
  432.4 30.9 %collective-permute-start.1 = (bf16[1,128,2048]{1,2,0:T(8,128)(2,1)S(1)}, bf16[1,128,2048]{1,2,0:T(8,128)(2,1)}, u32[]{:S(2)}, u32[]{:S(2)}) collective-permute-start(bf16[1,128,2048]{1,2,0:T(8,128)(2,1)S(1)} %bitcast.124), channel_id=1, source_target_pairs={{0,8},{4,12},{8,16},{12,20},{16,24},{20,28},{24,32},{28,36},{32,40... | collective-permute-start | bytes 1572872 | tf_op jit(solution)/shard_map/ppermute | solution.py:23
  434.4 33.9 %collective-permute-start.2 = (bf16[1,128,2048]{1,2,0:T(8,128)(2,1)S(1)}, bf16[1,128,2048]{1,2,0:T(8,128)(2,1)S(1)}, u32[]{:S(2)}, u32[]{:S(2)}) collective-permute-start(bf16[1,128,2048]{1,2,0:T(8,128)(2,1)S(1)} %bitcast.125), channel_id=1, source_target_pairs={{0,4},{4,8},{8,12},{12,16},{16,20},{20,24},{24,28},{28,32},{32,36}... | collective-permute-start | bytes 1572872 | tf_op jit(solution)/shard_map/ppermute | solution.py:23
  436.3 33.7 %collective-permute-start.3 = (bf16[1,128,2048]{1,2,0:T(8,128)(2,1)S(1)}, bf16[1,128,2048]{1,2,0:T(8,128)(2,1)S(1)}, u32[]{:S(2)}, u32[]{:S(2)}) collective-permute-start(bf16[1,128,2048]{1,2,0:T(8,128)(2,1)S(1)} %bitcast.126), channel_id=1, source_target_pairs={{4,0},{8,4},{12,8},{16,12},{20,16},{24,20},{28,24},{32,28},{36,32}... | collective-permute-start | bytes 1572872 | tf_op jit(solution)/shard_map/ppermute | solution.py:23
  443.3 29.6 %collective-permute-start.4 = (bf16[1,128,2048]{1,2,0:T(8,128)(2,1)S(1)}, bf16[1,128,2048]{1,2,0:T(8,128)(2,1)S(1)}, u32[]{:S(2)}, u32[]{:S(2)}) collective-permute-start(bf16[1,128,2048]{1,2,0:T(8,128)(2,1)S(1)} %bitcast.127), channel_id=1, source_target_pairs={{8,0},{12,4},{16,8},{20,12},{24,16},{28,20},{32,24},{36,28},{40,32... | collective-permute-start | bytes 1572872 | tf_op jit(solution)/shard_map/ppermute | solution.py:23
  447.5 0.7 copy-start.3
  451.3 40.0 %collective-permute-start.5 = (bf16[1,128,2048]{1,2,0:T(8,128)(2,1)S(1)}, bf16[1,128,2048]{1,2,0:T(8,128)(2,1)S(1)}, u32[]{:S(2)}, u32[]{:S(2)}) collective-permute-start(bf16[1,128,2048]{1,2,0:T(8,128)(2,1)S(1)} %bitcast.128), channel_id=1, source_target_pairs={{12,0},{16,4},{20,8},{24,12},{28,16},{32,20},{36,24},{40,28},{44,3... | collective-permute-start | bytes 1572872 | tf_op jit(solution)/shard_map/ppermute | solution.py:23
  503.1 2.9 copy-start.6
  506.0 0.8 copy-start.7
  508.4 1.0 copy-start.2
  509.3 207.7 %copy-start.4 = (f32[8,128,16]{1,2,0:T(8,128)S(1)}, f32[8,128,16]{1,2,0:T(8,128)}, u32[]{:S(2)}) copy-start(f32[8,128,16]{1,2,0:T(8,128)} %copy-done.3) | copy-start | bytes 196612
  509.3 207.7 %copy-start.5 = (pred[128,128]{1,0:T(8,128)(4,1)S(1)}, pred[128,128]{1,0:T(8,128)(4,1)}, u32[]{:S(2)}) copy-start(pred[128,128]{1,0:T(8,128)(4,1)} %iota_compare_fusion) | copy-start | bytes 49156
  509.3 207.7 %copy-start.13 = (f32[8,128,16]{1,2,0:T(8,128)S(1)}, f32[8,128,16]{1,2,0:T(8,128)}, u32[]{:S(2)}) copy-start(f32[8,128,16]{1,2,0:T(8,128)} %copy-done.12) | copy-start | bytes 196612
  509.3 207.7 %copy-start.15 = (f32[8,128]{1,0:T(8,128)S(1)}, f32[8,128]{1,0:T(8,128)}, u32[]{:S(2)}) copy-start(f32[8,128]{1,0:T(8,128)} %copy-done.14) | copy-start | bytes 12292
  509.5 208.1 %copy-start.8 = (f32[1024]{0:T(1024)S(1)}, f32[1024]{0:T(1024)}, u32[]{:S(2)}) copy-start(f32[1024]{0:T(1024)} %param.11) | copy-start | bytes 12292
  509.9 208.9 %copy-start.1 = (bf16[1,128,2048]{2,1,0:T(8,128)(2,1)S(1)}, bf16[1,128,2048]{2,1,0:T(8,128)(2,1)}, u32[]{:S(2)}) copy-start(bf16[1,128,2048]{2,1,0:T(8,128)(2,1)} %param.8) | copy-start | bytes 1572868
Sparse Core Ops, SparseCore 0:
  169.4 190.5 all-reduce.3
  363.2 141.1 all-gather.3
